TPU v7x, 1024 devices: a whole 4x4x32 slice. The times are simulated.
1024 devices in a mesh: expert: 32 (over z), dp: 32 (over x, y, core).
Axes of the slice: x: 4, y: 4, z: 32, core: 2. Of those that a mesh axis runs over, the one named last changes fastest.
Arguments:
- quant_in: bfloat16 [4096, 7168], P('expert', 'dp'), may hold values from -4 to 4
- quant_scale: float32 [4096, 56], P('expert'), may hold values from 0.25 to 4
- grad_out: bfloat16 [4096, 7168], P('expert', 'dp'), may hold values from -6 to 6
- route_ids: int32 [4096, 1], replicated, may hold values from 0 to 31; in each aligned block of 128 rows (0 to 127, 128 to 255, ...) at most 12 rows name the same one
- route_weights: float32 [4096, 1], replicated, may hold values from 0.1 to 1
- w_gate: bfloat16 [32, 7168, 1024], P('expert', 'dp'), may hold values from -0.0625 to 0.0625
- w_up: bfloat16 [32, 7168, 1024], P('expert', 'dp'), may hold values from -0.0625 to 0.0625
- w_down: bfloat16 [32, 1024, 7168], P('expert', None, 'dp'), may hold values from -0.1875 to 0.1875
Outputs:
- grad_in: bfloat16 [4096, 7168], P('expert', 'dp')
- grad_gate: bfloat16 [32, 7168, 1024], P('expert', 'dp')
- grad_up: bfloat16 [32, 7168, 1024], P('expert', 'dp')
- grad_down: bfloat16 [32, 1024, 7168], P('expert', None, 'dp')
Inputs may be any that keep to these rules, and one draw needn't show every extreme that they name: `route_ids`: each token names 1 different experts. Among the 128 tokens of one aligned group, no expert is named more than 12 times, a bound that some block reaches.
All inputs are finite; a program needn't handle non-finite values.
Results may differ from a plain program's by a relative error of at most 0.0076.
Values may be sent and summed in bfloat16 or wider, within the bound.
A program may use at most 64 MiB of HBM per device.

v0:
```python
import jax
import jax.numpy as jnp
from jax import lax
from jax.sharding import PartitionSpec as P

D = 7168
E = 32
K = 1
QB = 128
TOK_E = 128
CAP = 12


def slot_tables(route_rows, weights):
    expert_ids = jnp.arange(E, dtype=jnp.int32)
    matches = route_rows[:, :, None] == expert_ids[None, None, :]
    member = jnp.sum(matches.astype(jnp.int32), axis=1)
    chosen = jnp.sum(
        jnp.where(matches, weights[:, :, None], jnp.zeros_like(weights)[:, :, None]), axis=1
    )
    earlier = jnp.cumsum(member, axis=0) - member
    places = jnp.arange(CAP, dtype=jnp.int32)
    select = (member.T[:, None, :] == 1) & (earlier.T[:, None, :] == places[None, :, None])
    slot_weight = jnp.sum(
        jnp.where(select, chosen.T[:, None, :], jnp.zeros_like(chosen).T[:, None, :]), axis=2
    )
    return (select, slot_weight)


def gated_backward(summed):
    gate_sum = summed[..., 0, :]
    up_sum = summed[..., 1, :]
    down_sum = summed[..., 2, :]
    sigma = jax.nn.sigmoid(gate_sum)
    hidden = gate_sum * sigma * up_sum
    grad_gate_in = down_sum * up_sum * sigma * (1.0 + gate_sum * (1.0 - sigma))
    grad_up_in = down_sum * gate_sum * sigma
    return jnp.stack((hidden, grad_gate_in, grad_up_in), axis=-2).astype(jnp.bfloat16)


def on_device(quant_in, quant_scale, grad_out, route_ids, route_weights, w_gate, w_up, w_down):
    groups = lax.axis_size("expert")
    local_count = w_gate.shape[0]
    slice_width = w_gate.shape[1]
    slot_count = groups * CAP
    expert_rank = lax.axis_index("expert")
    column_start = lax.axis_index("dp") * slice_width
    columns = column_start + jnp.arange(slice_width, dtype=jnp.int32)
    block_ids = jnp.arange(D // QB, dtype=jnp.int32)
    picker = (block_ids[:, None] == (columns // QB)[None, :]).astype(jnp.float32)
    column_scale = jnp.dot(
        quant_scale, picker, precision=lax.Precision.HIGHEST, preferred_element_type=jnp.float32
    )
    rows_in = (quant_in.astype(jnp.float32) * column_scale).astype(jnp.bfloat16)
    select, slot_weight = jax.vmap(slot_tables)(
        route_ids.reshape(groups, TOK_E, K), route_weights.reshape(groups, TOK_E, K)
    )
    first_local = expert_rank * local_count
    mine_weight = lax.dynamic_slice_in_dim(slot_weight, first_local, local_count, 1)
    slot_scale = jnp.transpose(mine_weight, (1, 0, 2)).reshape(local_count, slot_count)
    own_select = lax.dynamic_index_in_dim(select, expert_rank, 0, keepdims=False).astype(
        jnp.bfloat16
    )
    send_x = jnp.einsum(
        "ect,td->ecd", own_select, rows_in, preferred_element_type=jnp.float32
    ).astype(jnp.bfloat16)
    send_grad = jnp.einsum(
        "ect,td->ecd", own_select, grad_out, preferred_element_type=jnp.float32
    ).astype(jnp.bfloat16)
    recv_x, recv_grad = (
        lax.all_to_all(send_x, "expert", split_axis=0, concat_axis=1, tiled=True),
        lax.all_to_all(send_grad, "expert", split_axis=0, concat_axis=1, tiled=True),
    )
    scaled_grad = (slot_scale[:, :, None] * recv_grad.astype(jnp.float32)).astype(jnp.bfloat16)
    gate_sum = jnp.einsum("nrd,ndh->rnh", recv_x, w_gate, preferred_element_type=jnp.float32)
    up_sum = jnp.einsum("nrd,ndh->rnh", recv_x, w_up, preferred_element_type=jnp.float32)
    down_sum = jnp.einsum("nrd,nhd->rnh", scaled_grad, w_down, preferred_element_type=jnp.float32)
    summed = lax.psum_scatter(
        jnp.stack((gate_sum, up_sum, down_sum), axis=2), "dp", scatter_dimension=0, tiled=True
    )
    values = lax.all_gather(gated_backward(summed), "dp", axis=0, tiled=True)
    hidden = values[:, :, 0, :]
    grad_gate_in = values[:, :, 1, :]
    grad_up_in = values[:, :, 2, :]
    grad_gate = jnp.einsum(
        "nrd,rnh->ndh", recv_x, grad_gate_in, preferred_element_type=jnp.float32
    ).astype(jnp.bfloat16)
    grad_up = jnp.einsum(
        "nrd,rnh->ndh", recv_x, grad_up_in, preferred_element_type=jnp.float32
    ).astype(jnp.bfloat16)
    grad_down = jnp.einsum(
        "rnh,nrd->nhd", hidden, scaled_grad, preferred_element_type=jnp.float32
    ).astype(jnp.bfloat16)
    returned = jnp.einsum("rnh,ndh->nrd", grad_gate_in, w_gate, preferred_element_type=jnp.float32)
    returned = returned + jnp.einsum(
        "rnh,ndh->nrd", grad_up_in, w_up, preferred_element_type=jnp.float32
    )
    arrived = lax.all_to_all(
        returned.astype(jnp.bfloat16), "expert", split_axis=1, concat_axis=0, tiled=True
    )
    grad_in = jnp.einsum(
        "ect,ecd->td", own_select, arrived, preferred_element_type=jnp.float32
    ).astype(jnp.bfloat16)
    return (grad_in, grad_gate, grad_up, grad_down)


def solution(mesh):
    placed = (
        P("expert", "dp"),
        P("expert", None),
        P("expert", "dp"),
        P(),
        P(),
        P("expert", "dp", None),
        P("expert", "dp", None),
        P("expert", None, "dp"),
    )
    return jax.shard_map(
        on_device,
        mesh=mesh,
        in_specs=placed,
        out_specs=(
            P("expert", "dp"),
            P("expert", "dp", None),
            P("expert", "dp", None),
            P("expert", None, "dp"),
        ),
        check_vma=False,
    )
```

profile of v0, /device:TPU:1, one launch (start us, length us, event | category | flops | bytes accessed | tf_op | source)
XLA Modules:
  0.0 483.7 jit_solution(16837854681490852063)
XLA Ops:
  9.2 2.0 convert_compare_fusion
  11.2 1.3 copy.46
  12.4 2.4 copy.44
  17.3 29.3 %all-to-all-start = ((bf16[32,12,224]{2,1,0:T(8,128)(2,1)}), bf16[32,12,224]{2,1,0:T(8,128)(2,1)S(1)}, u32[]{:S(2)}, u32[]{:S(2)}) async-start(bf16[32,12,224]{2,1,0:T(8,128)(2,1)} %copy.47), calls=%async_computation | async-start | bytes 524288 | tf_op jit(solution)/shard_map/all_to_all | solution.py:71
  47.7 39.4 %all-to-all-done = bf16[32,12,224]{2,1,0:T(8,128)(2,1)S(1)} async-done(((bf16[32,12,224]{2,1,0:T(8,128)(2,1)}), bf16[32,12,224]{2,1,0:T(8,128)(2,1)S(1)}, u32[]{:S(2)}, u32[]{:S(2)}) %all-to-all-start) | async-done | bytes 172064 | tf_op jit(solution)/shard_map/all_to_all | solution.py:71
  87.2 4.6 all-to-all-start.1
  92.7 2.0 fusion.3
  94.7 2.1 copy.49
  96.8 2.8 select_reduce_fusion
  100.5 1.5 convolution_bitcast_fusion.2
  102.0 27.5 %all-to-all-done.1 = bf16[32,12,224]{2,1,0:T(8,128)(2,1)} async-done(((bf16[32,12,224]{2,1,0:T(8,128)(2,1)}), bf16[32,12,224]{2,1,0:T(8,128)(2,1)}, u32[]{:S(2)}, u32[]{:S(2)}) %all-to-all-start.1) | async-done | bytes 172064 | tf_op jit(solution)/shard_map/all_to_all | solution.py:72
  132.0 2.8 pad_maximum_fusion
  134.7 9.3 %copy.52 = f32[384,1,3,1024]{3,1,2,0:T(1,128)} copy(f32[384,1,3,1024]{3,0,2,1:T(8,128)} %pad_maximum_fusion) | data formatting | bytes 9437184 | tf_op jit(solution)/shard_map/stack | solution.py:79
  144.3 1.3 dynamic-slice
  146.3 169.1 %all-reduce.3.cloned.1.call-done = f32[384,1,3,1024]{3,1,2,0:T(1,128)} async-done(((f32[384,1,3,1024]{3,1,2,0:T(1,128)}), f32[384,1,3,1024]{3,1,2,0:T(1,128)}) %all-reduce.3.cloned.1.call-update) | async-done | bytes 4718608
  318.3 84.0 %all-gather.2.cloned.1.call-done = bf16[384,1,3,1024]{3,2,1,0:T(4,128)(2,1)} async-done(((bf16[12,1,3,1024]{3,2,1,0:T(4,128)(2,1)}), bf16[384,1,3,1024]{3,2,1,0:T(4,128)(2,1)}) %all-gather.2.cloned.1.call-update) | async-done | bytes 2359312 | tf_op jit(solution)/shard_map/all_gather | solution.py:81
  402.3 7.9 %fusion.37 = (bf16[384,1,1,1024]{3,2,1,0:T(2,128)(2,1)S(1)}, bf16[384,1,1,1024]{3,2,1,0:T(2,128)(2,1)S(1)}, bf16[384,1,1,1024]{3,2,1,0:T(2,128)(2,1)S(1)}) fusion(bf16[384,1,3,1024]{3,2,1,0:T(4,128)(2,1)} %all-gather.2.cloned.1.call-done), kind=kLoop, calls=%fused_computation.67 | loop fusion | bytes 4718592 | tf_op jit(solution)/shard_map/slice | solution.py:82
  413.5 1.9 reduce.4
  416.4 22.6 %all-to-all-start.2 = ((bf16[32,2,1344]{2,1,0:T(2,128)(2,1)}), bf16[32,2,1344]{2,1,0:T(2,128)(2,1)S(1)}, u32[]{:S(2)}, u32[]{:S(2)}) async-start(bf16[32,2,1344]{2,1,0:T(2,128)(2,1)} %reshape.267), calls=%async_computation.2 | async-start | bytes 360448 | tf_op jit(solution)/shard_map/all_to_all | solution.py:98
  439.1 2.7 fusion.7
  441.7 2.7 fusion.6
  444.4 1.3 fusion.8
  445.7 27.9 %all-to-all-done.2 = bf16[32,2,1344]{2,1,0:T(2,128)(2,1)S(1)} async-done(((bf16[32,2,1344]{2,1,0:T(2,128)(2,1)}), bf16[32,2,1344]{2,1,0:T(2,128)(2,1)S(1)}, u32[]{:S(2)}, u32[]{:S(2)}) %all-to-all-start.2) | async-done | bytes 172064 | tf_op jit(solution)/shard_map/all_to_all | solution.py:98
  475.1 1.7 fusion.13
  (56 shorter events, 18.7 us)
Async XLA Ops:
  7.2 93.3 %copy-start = (bf16[1,224,1024]{2,1,0:T(8,128)(2,1)S(1)}, bf16[1,224,1024]{2,1,0:T(8,128)(2,1)}, u32[]{:S(2)}) copy-start(bf16[1,224,1024]{2,1,0:T(8,128)(2,1)} %param.13) | copy-start | bytes 1376260
  12.4 3.5 copy-start.9
  12.4 3.5 copy-start.10
  14.8 31.8 %copy-start.8 = (bf16[128,224]{0,1:T(8,128)(2,1)S(1)}, bf16[128,224]{0,1:T(8,128)(2,1)}, u32[]{:S(2)}) copy-start(bf16[128,224]{0,1:T(8,128)(2,1)} %param.10) | copy-start | bytes 172036
  16.0 76.0 %copy-start.4 = (pred[32,32,12,128]{3,1,2,0:T(32,128)(4,1)}, pred[32,32,12,128]{3,1,2,0:T(32,128)(4,1)S(1)}, u32[]{:S(2)}) copy-start(pred[32,32,12,128]{3,1,2,0:T(32,128)(4,1)S(1)} %fusion) | copy-start | bytes 4718596
  16.0 76.0 %copy-start.11 = (f32[4096,1]{0,1:T(1,128)S(1)}, f32[4096,1]{0,1:T(1,128)}, u32[]{:S(2)}) copy-start(f32[4096,1]{0,1:T(1,128)} %param.12) | copy-start | bytes 49156
  17.3 69.8 %all-to-all-start = ((bf16[32,12,224]{2,1,0:T(8,128)(2,1)}), bf16[32,12,224]{2,1,0:T(8,128)(2,1)S(1)}, u32[]{:S(2)}, u32[]{:S(2)}) async-start(bf16[32,12,224]{2,1,0:T(8,128)(2,1)} %copy.47), calls=%async_computation | async-start | bytes 524288 | tf_op jit(solution)/shard_map/all_to_all | solution.py:71
  87.2 42.4 %all-to-all-start.1 = ((bf16[32,12,224]{2,1,0:T(8,128)(2,1)}), bf16[32,12,224]{2,1,0:T(8,128)(2,1)}, u32[]{:S(2)}, u32[]{:S(2)}) async-start(bf16[32,12,224]{2,1,0:T(8,128)(2,1)} %copy.50), calls=%async_computation.1 | async-start | bytes 524288 | tf_op jit(solution)/shard_map/all_to_all | solution.py:72
  91.7 223.6 %all-reduce.3.cloned.1.call-start = ((), (), s32[]{:S(2)}) async-start(), calls=%async_computation.4 | async-start | bytes 9437184
  96.8 3.3 copy-start.6
  100.4 30.1 %copy-start.5 = (bf16[1,1024,224]{1,2,0:T(8,128)(2,1)S(1)}, bf16[1,1024,224]{1,2,0:T(8,128)(2,1)}, u32[]{:S(2)}) copy-start(bf16[1,1024,224]{1,2,0:T(8,128)(2,1)} %param.15) | copy-start | bytes 1376260
  130.5 1.4 copy-start.1
  144.1 258.2 %all-gather.2.cloned.1.call-start = ((), (), s32[]{:S(2)}) async-start(), calls=%async_computation.3 | async-start | bytes 3244032 | tf_op jit(solution)/shard_map/all_gather | solution.py:81
  410.2 1.1 copy-start.2
  410.2 1.6 copy-start.3
  410.2 1.6 copy-start.7
  416.4 57.2 %all-to-all-start.2 = ((bf16[32,2,1344]{2,1,0:T(2,128)(2,1)}), bf16[32,2,1344]{2,1,0:T(2,128)(2,1)S(1)}, u32[]{:S(2)}, u32[]{:S(2)}) async-start(bf16[32,2,1344]{2,1,0:T(2,128)(2,1)} %reshape.267), calls=%async_computation.2 | async-start | bytes 360448 | tf_op jit(solution)/shard_map/all_to_all | solution.py:98
Sparse Core Ops, SparseCore 0:
  144.2 171.1 all-reduce.2
  321.0 81.2 all-gather.1
where the time goes:
time: 485 us; the launch traced here: 484 us
  waiting for transfers between devices  348 us (72%)
  starting transfers between devices  57 us (12%)
  local copies, waits for them, and re-layouts  35.5 us (7%)
  other arithmetic  15.8 us (3%)
  between operations  15 us (3%)
  matrix products  12.3 us (3%)
    unnamed x3, waiting for transfers between devices  169 us
    all_gather x1, waiting for transfers between devices, on_device(): values = lax.all_gather(gated_backward(summed), 'dp', axis=0, tiled=True)  84 us
    all_to_all x1, waiting for transfers between devices, on_device(): lax.all_to_all(send_x, 'expert', split_axis=0, concat_axis=1, tiled=True)  39.4 us
    all_to_all x1, starting transfers between devices, on_device(): lax.all_to_all(send_x, 'expert', split_axis=0, concat_axis=1, tiled=True)  29.3 us
    all_to_all x1, waiting for transfers between devices, on_device(): lax.all_to_all(returned.astype(jnp.bfloat16), 'expert', split_axis=1, con...  27.9 us
    all_to_all x1, waiting for transfers between devices, on_device(): lax.all_to_all(send_grad, 'expert', split_axis=0, concat_axis=1, tiled=True)  27.5 us
    all_to_all x1, starting transfers between devices, on_device(): lax.all_to_all(returned.astype(jnp.bfloat16), 'expert', split_axis=1, con...  22.6 us
  transfers between devices with their start and end apart: 5, of which 5 were waited for; matrix products, arithmetic and copies ran while one was open for 4% of the time, Pallas kernels for 0%

commit v1 on v0

v1 whole, which is shorter than its diff:
```python
import functools

import jax
import jax.numpy as jnp
from jax import lax
from jax.experimental import pallas as pl
from jax.experimental.pallas import tpu as pltpu
from jax.sharding import PartitionSpec as P

MESH = pl.DeviceIdType.MESH
F32 = jnp.float32
BF16 = jnp.bfloat16

D = 7168
H = 1024
QB = 128
TOK = 128
CAP = 12
Z = 32
SIDE = 4
W = 224
HALF = H // 2
SLOT = 16
WIDE = 384
ROWS = Z * CAP
TYPE = ROWS // 2
BLK = TYPE // SIDE
LANES = HALF // SIDE
GROUP = 8


def dot(a, b, dims=((1,), (0,))):
    return lax.dot_general(a, b, (dims, ((), ())), preferred_element_type=F32)


def iota(shape, dim):
    return lax.broadcasted_iota(jnp.int32, shape, dim)


def one_hot(cond):
    return jnp.where(cond, 1.0, 0.0).astype(BF16)


def hop(p):
    return 16 + ((p + 1) // 2) * (1 - 2 * (p % 2))


def to_column(row):
    diag = iota((TOK, TOK), 0) == iota((TOK, TOK), 1)
    spread = jnp.broadcast_to(row, (TOK, TOK))
    return jnp.sum(jnp.where(diag, spread, jnp.zeros_like(spread)), axis=1, keepdims=True)


def kernel(
    quant_ref, scale_ref, grad_ref, ids_ref, wts_ref, wg_hbm, wu_hbm, wd_hbm,
    gin_ref, gg_hbm, gu_hbm, gd_hbm,
    send, recv, recvp, pick, wg, wu, wd, wgp, wup, wdp, xo, xp, go, gp,
    part, rx1, sum1, rx2, val, rsend, rrecv, gg, gu, gd,
    zs, zr, fs, fr, ws, wr, wl, cs, cr, ps, pr, bs, br, os,
):
    z = lax.axis_index("expert")
    d = lax.axis_index("dp")
    cx, cy, core = d // 8, (d // 2) % 4, d % 2
    mate = {"dp": d + 1 - 2 * core}

    def at_x(j):
        return {"dp": (((cx + j) % 4) * 4 + cy) * 2 + core}

    def at_y(j):
        return {"dp": (cx * 4 + (cy + j) % 4) * 2 + core}

    def remote(src, dst, s, r, device):
        return pltpu.make_async_remote_copy(
            src_ref=src, dst_ref=dst, send_sem=s, recv_sem=r, device_id=device, device_id_type=MESH
        )

    barrier = pltpu.get_barrier_semaphore()

    def greet(k, carry):
        pl.semaphore_signal(
            barrier, inc=1, device_id={"expert": (z + k) % Z}, device_id_type=MESH
        )
        return carry

    lax.fori_loop(1, Z, greet, 0)
    for device in [mate] + [at_x(j) for j in (1, 2, 3)] + [at_y(j) for j in (1, 2, 3)]:
        pl.semaphore_signal(barrier, inc=1, device_id=device, device_id_type=MESH)

    local = [
        pltpu.make_async_copy(wg_hbm, wg, wl.at[0]),
        pltpu.make_async_copy(wu_hbm, wu, wl.at[1]),
        pltpu.make_async_copy(wd_hbm, wd, wl.at[2]),
    ]
    for c in local:
        c.start()

    ids = ids_ref[pl.ds(z, 1), :]
    member = one_hot(iota((Z, TOK), 0) == jnp.broadcast_to(ids, (Z, TOK)))
    before = one_hot(iota((TOK, TOK), 0) < iota((TOK, TOK), 1))
    earlier = dot(member, before)
    slot = jnp.sum(member.astype(F32) * earlier, axis=0, keepdims=True).astype(jnp.int32)
    k = (ids - z) & (Z - 1)
    place = SLOT * jnp.where(k < 16, 31 - 2 * k, 2 * k - 32)
    late = jnp.where(slot >= 6, 1, 0)
    rows = iota((Z * SLOT, TOK), 0)
    pick_main = one_hot(rows == jnp.broadcast_to(place + slot, (Z * SLOT, TOK)))
    pick_tail = one_hot(rows == jnp.broadcast_to(place + CAP + late, (Z * SLOT, TOK)))
    pick[...] = pick_main
    sixth = to_column(slot - 6 * late)
    weight = to_column(wts_ref[pl.ds(z, 1), :])

    picker = jnp.where(
        iota((D // QB, W), 0) == ((W * d + iota((D // QB, W), 1)) >> 7), 1.0, 0.0
    ).astype(F32)
    col_scale = jnp.dot(
        scale_ref[...], picker, precision=lax.Precision.HIGHEST, preferred_element_type=F32
    )
    x = (quant_ref[...].astype(F32) * col_scale).astype(BF16)
    g = (grad_ref[...].astype(F32) * weight).astype(BF16)
    r, c = iota((W, WIDE), 0), iota((W, WIDE), 1)
    put_x = one_hot(r == c)
    put_g = one_hot(((c >= 256) & (r == c - 256)) | ((c >= W) & (c < 256) & (r == c - 96)))
    put_t = one_hot(r == 160 + (c & 63))
    wide = (dot(x, put_x) + dot(g, put_g)).astype(BF16)
    tail = dot(g, put_t)
    tail = jnp.where((iota((TOK, WIDE), 1) >> 6) == sixth, tail, 0.0).astype(BF16)
    for q in range(4):
        at = pl.ds(128 * q, 128)
        send[at, :] = (
            dot(pick_main[128 * q : 128 * q + 128], wide)
            + dot(pick_tail[128 * q : 128 * q + 128], tail)
        ).astype(BF16)

    pl.semaphore_wait(barrier, Z - 1 + 7)

    def block(p):
        return pl.ds(pl.multiple_of(p * SLOT, SLOT), SLOT)

    def out_copy(p):
        return remote(
            send.at[block(p)], recv.at[block(p)], zs.at[p], zr.at[p],
            {"expert": (z + hop(p)) % Z},
        )

    def start_out(p, carry):
        out_copy(p).start()
        return carry

    lax.fori_loop(0, Z - 1, start_out, 0)
    recv[pl.ds((Z - 1) * SLOT, SLOT), :] = send[pl.ds((Z - 1) * SLOT, SLOT), :]

    other = pl.ds(pl.multiple_of((1 - core) * HALF, HALF), HALF)
    mine = pl.ds(pl.multiple_of(core * HALF, HALF), HALF)
    weights_out = [
        remote(wg_hbm.at[:, other], wgp, ws.at[0], wr.at[0], mate),
        remote(wu_hbm.at[:, other], wup, ws.at[1], wr.at[1], mate),
        remote(wd_hbm.at[other, :], wdp, ws.at[2], wr.at[2], mate),
    ]
    for c in weights_out:
        c.start()

    gr = GROUP * CAP
    i, j = iota((gr, 128), 0), iota((gr, 128), 1)
    src, cc = j >> 4, j & 15
    take_main = one_hot((cc < CAP) & (i == CAP * src + cc))
    off = i - CAP * src - 6 * (cc - CAP)
    take_tail = one_hot((cc >= CAP) & (cc < CAP + 2) & (off >= 0) & (off < 6))
    ri = iota((gr, WIDE), 0)
    tail_lane = (iota((gr, WIDE), 1) >> 6) == ri - 6 * ((ri * 43) >> 8)
    r, c = iota((WIDE, W), 0), iota((WIDE, W), 1)
    get_g = one_hot(((c < 128) & (r == c + 256)) | ((c >= 128) & (c < 160) & (r == c + 96)))
    get_t = one_hot((c >= 160) & (c - 160 == (r & 63)))

    def unpack(ref, q, x_ref, g_ref):
        raw = ref[pl.ds(128 * q, 128), :]
        main = dot(take_main, raw).astype(BF16)
        ends = jnp.where(tail_lane, dot(take_tail, raw), 0.0).astype(BF16)
        x_ref[pl.ds(gr * q, gr), :] = main[:, :W]
        g_ref[pl.ds(gr * q, gr), :] = (dot(main, get_g) + dot(ends, get_t)).astype(BF16)

    def forward_copy(q):
        at = pl.ds(128 * q, 128)
        return remote(recv.at[at], recvp.at[at], fs.at[q], fr.at[q], mate)

    def arrive(p, carry):
        out_copy(p).wait_recv()
        return carry

    first = (cx, cy)
    second = (cy, cx)
    peer1 = (at_x, at_y)
    peer2 = (at_y, at_x)

    def rows_of(t, a):
        return pl.ds(pl.multiple_of(TYPE * t + BLK * a, 16), BLK)

    def lanes_of(b):
        return pl.ds(pl.multiple_of(LANES * b, LANES), LANES)

    def rs1(t, j):
        a = (first[t] + j) % 4
        return remote(
            part.at[:, rows_of(t, a), :], rx1.at[t, j - 1], cs.at[0, t, j - 1], cr.at[0, t, j - 1],
            peer1[t](j),
        )

    def rs2(t, j):
        b = (second[t] + j) % 4
        return remote(
            sum1.at[t, :, :, lanes_of(b)], rx2.at[t, j - 1], cs.at[1, t, j - 1],
            cr.at[1, t, j - 1], peer2[t](j),
        )

    def ag2(t, j, back=0):
        ref = val.at[core, :, rows_of(t, first[t]), lanes_of((second[t] + 4 - back) % 4)]
        return remote(ref, ref, cs.at[2, t, j - 1], cr.at[2, t, j - 1], peer2[t](j))

    def ag1(t, j, back=0):
        ref = val.at[core, :, rows_of(t, (first[t] + 4 - back) % 4), :]
        return remote(ref, ref, cs.at[3, t, j - 1], cr.at[3, t, j - 1], peer1[t](j))

    def pair(t, half):
        ref = val.at[half, :, pl.ds(TYPE * t, TYPE), :]
        return remote(ref, ref, ps.at[t], pr.at[t], mate)

    peers = (1, 2, 3)

    def products(t):
        at = pl.ds(TYPE * t, TYPE)
        nt = ((1,), (1,))
        a, b = xo[at, :], xp[at, :]
        part[0, at, :] = (dot(a, wg[:, mine]) + dot(b, wgp[...])).astype(BF16)
        part[1, at, :] = (dot(a, wu[:, mine]) + dot(b, wup[...])).astype(BF16)
        a, b = go[at, :], gp[at, :]
        part[2, at, :] = (dot(a, wd[mine, :], nt) + dot(b, wdp[...], nt)).astype(BF16)

    for t in (0, 1):
        for q in (2 * t, 2 * t + 1):
            lax.fori_loop(GROUP * q, min(GROUP * q + GROUP, Z - 1), arrive, 0)
            forward_copy(q).start()
        if t == 0:
            for c in local:
                c.wait()
            for c in weights_out:
                c.wait_recv()
        for q in (2 * t, 2 * t + 1):
            unpack(recv, q, xo, go)
            forward_copy(q).wait_recv()
            unpack(recvp, q, xp, gp)
        products(t)
        for j in peers:
            rs1(t, j).start()

    for t in (0, 1):
        for j in peers:
            rs1(t, j).wait_recv()
        total = part[:, rows_of(t, first[t]), :].astype(F32)
        for j in peers:
            total = total + rx1[t, j - 1].astype(F32)
        sum1[t] = total.astype(BF16)
        for j in peers:
            rs2(t, j).start()

    for t in (0, 1):
        for j in peers:
            rs2(t, j).wait_recv()
        total = sum1[t, :, :, lanes_of(second[t])].astype(F32)
        for j in peers:
            total = total + rx2[t, j - 1].astype(F32)
        gate, up, down = total[0], total[1], total[2]
        sigma = jax.nn.sigmoid(gate)
        at, lanes = rows_of(t, first[t]), lanes_of(second[t])
        val[core, 0, at, lanes] = (gate * sigma * up).astype(BF16)
        val[core, 1, at, lanes] = (
            down * up * sigma * (1.0 + gate * (1.0 - sigma))
        ).astype(BF16)
        val[core, 2, at, lanes] = (down * gate * sigma).astype(BF16)
        for j in peers:
            ag2(t, j).start()

    for t in (0, 1):
        for j in peers:
            ag2(t, j, j).wait_recv()
        for j in peers:
            ag1(t, j).start()

    for t in (0, 1):
        for j in peers:
            ag1(t, j, j).wait_recv()
        pair(t, core).start()

    i, j = iota((128, gr), 0), iota((128, gr), 1)
    spread = one_hot(((i & 15) < CAP) & (j == CAP * (i >> 4) + (i & 15)))

    def back_copy(p):
        return remote(
            rsend.at[block(p)], rrecv.at[block(p)], bs.at[p], br.at[p],
            {"expert": (z + Z - hop(p)) % Z},
        )

    def start_back(p, carry):
        back_copy(p).start()
        return carry

    nt = ((1,), (1,))
    for t in (0, 1):
        pair(t, 1 - core).wait_recv()
        at = pl.ds(TYPE * t, TYPE)
        slots = (
            dot(val[0, 1, at, :], wg[:, :HALF], nt)
            + dot(val[1, 1, at, :], wg[:, HALF:], nt)
            + dot(val[0, 2, at, :], wu[:, :HALF], nt)
            + dot(val[1, 2, at, :], wu[:, HALF:], nt)
        ).astype(BF16)
        for q in (0, 1):
            rsend[pl.ds(256 * t + 128 * q, 128), :] = dot(
                spread, slots[gr * q : gr * q + gr]
            ).astype(BF16)
        lax.fori_loop(16 * t, min(16 * t + 16, Z - 1), start_back, 0)
    rrecv[pl.ds((Z - 1) * SLOT, SLOT), :] = rsend[pl.ds((Z - 1) * SLOT, SLOT), :]

    tn = ((0,), (0,))
    for h in (0, 1):
        at = pl.ds(HALF * h, HALF)
        gg[:, at] = dot(xo[...], val[h, 1], tn).astype(BF16)
        gu[:, at] = dot(xo[...], val[h, 2], tn).astype(BF16)
        gd[at, :] = dot(val[h, 0], go[...], tn).astype(BF16)
    outs = [
        pltpu.make_async_copy(gg, gg_hbm, os.at[0]),
        pltpu.make_async_copy(gu, gu_hbm, os.at[1]),
        pltpu.make_async_copy(gd, gd_hbm, os.at[2]),
    ]
    for c in outs:
        c.start()

    def home(p, carry):
        back_copy(p).wait_recv()
        return carry

    lax.fori_loop(0, Z - 1, home, 0)
    gin_ref[...] = dot(pick[...], rrecv[...], tn).astype(BF16)

    def drain(p, carry):
        out_copy(p).wait_send()
        back_copy(p).wait_send()
        return carry

    lax.fori_loop(0, Z - 1, drain, 0)
    for c in weights_out:
        c.wait_send()
    for q in range(4):
        forward_copy(q).wait_send()
    for t in (0, 1):
        pair(t, core).wait_send()
        for j in peers:
            rs1(t, j).wait_send()
            rs2(t, j).wait_send()
            ag2(t, j).wait_send()
            ag1(t, j).wait_send()
    for c in outs:
        c.wait()


def on_device(quant_in, quant_scale, grad_out, route_ids, route_weights, w_gate, w_up, w_down):
    vmem = pl.BlockSpec(memory_space=pltpu.VMEM)
    hbm = pl.BlockSpec(memory_space=pl.ANY)
    dma = pltpu.SemaphoreType.DMA
    shapes = [
        ((Z * SLOT, WIDE), BF16), ((Z * SLOT, WIDE), BF16), ((Z * SLOT, WIDE), BF16),
        ((Z * SLOT, TOK), BF16),
        ((W, H), BF16), ((W, H), BF16), ((H, W), BF16),
        ((W, HALF), BF16), ((W, HALF), BF16), ((HALF, W), BF16),
        ((ROWS, W), BF16), ((ROWS, W), BF16), ((ROWS, W), BF16), ((ROWS, W), BF16),
        ((3, ROWS, HALF), BF16),
        ((2, 3, 3, BLK, HALF), BF16), ((2, 3, BLK, HALF), BF16), ((2, 3, 3, BLK, LANES), BF16),
        ((2, 3, ROWS, HALF), BF16),
        ((Z * SLOT, W), BF16), ((Z * SLOT, W), BF16),
        ((W, H), BF16), ((W, H), BF16), ((H, W), BF16),
    ]
    sems = [
        (Z - 1,), (Z - 1,), (4,), (4,), (3,), (3,), (3,), (4, 2, 3), (4, 2, 3), (2,), (2,),
        (Z - 1,), (Z - 1,), (3,),
    ]
    out_shape = [
        jax.ShapeDtypeStruct((TOK, W), BF16),
        jax.ShapeDtypeStruct((W, H), BF16),
        jax.ShapeDtypeStruct((W, H), BF16),
        jax.ShapeDtypeStruct((H, W), BF16),
    ]
    gin, gg, gu, gd = pl.pallas_call(
        kernel,
        out_shape=out_shape,
        in_specs=[vmem] * 5 + [hbm] * 3,
        out_specs=[vmem] + [hbm] * 3,
        scratch_shapes=[pltpu.VMEM(s, t) for s, t in shapes] + [dma(s) for s in sems],
        compiler_params=pltpu.CompilerParams(
            collective_id=0, has_side_effects=True, vmem_limit_bytes=48 * 1024 * 1024
        ),
        cost_estimate=pl.CostEstimate(
            flops=2 * 8 * ROWS * W * H, bytes_accessed=12 * W * H, transcendentals=ROWS * H // 32
        ),
    )(
        quant_in, quant_scale, grad_out,
        route_ids.reshape(Z, TOK), route_weights.reshape(Z, TOK),
        w_gate[0], w_up[0], w_down[0],
    )
    return gin, gg[None], gu[None], gd[None]


def solution(mesh):
    placed = (
        P("expert", "dp"),
        P("expert", None),
        P("expert", "dp"),
        P(),
        P(),
        P("expert", "dp", None),
        P("expert", "dp", None),
        P("expert", None, "dp"),
    )
    return jax.shard_map(
        on_device,
        mesh=mesh,
        in_specs=placed,
        out_specs=(
            P("expert", "dp"),
            P("expert", "dp", None),
            P("expert", "dp", None),
            P("expert", None, "dp"),
        ),
        check_vma=False,
    )
```

time: 485 us -> 131 us (0.27)
  waiting for transfers between devices: 348 us -> 0 us
  Pallas kernels: 0 us -> 123 us
  starting transfers between devices: 57 us -> 0 us
  local copies, waits for them, and re-layouts: 35.5 us -> 6.39 us
  other arithmetic: 15.8 us -> 0 us
  between operations: 15 us -> 0.75 us
  matrix products: 12.3 us -> 0 us
    unnamed x3 -> x0, waiting for transfers between devices: 169 us -> none
    pallas_call x0 -> x1, Pallas kernels: none -> 123 us  [on_device(): pl.pallas_call(kernel, out_shape=out_shape, in_specs=[vmem] * 5 + [hbm] *...]
    all_to_all x3 -> x0, waiting for transfers between devices: 94.9 us -> none  [the longest x1 39.4 us: on_device(): lax.all_to_all(send_x, 'expert', split_axis=0, concat_axis=1, tiled=True)]
    all_gather x1 -> x0, waiting for transfers between devices: 84 us -> none  [on_device(): values = lax.all_gather(gated_backward(summed), 'dp', axis=0, tiled=True)]
    all_to_all x3 -> x0, starting transfers between devices: 56.5 us -> none  [the longest x1 29.3 us: on_device(): lax.all_to_all(send_x, 'expert', split_axis=0, concat_axis=1, tiled=True)]
    dot_general x12 -> x0, matrix products: 12.3 us -> none  [the longest x1 2.66 us: on_device(): jnp.einsum('nrd,rnh->ndh', recv_x, grad_gate_in, preferred_element_type=j...]
    another operation x3 -> x0, local copies, waits for them, and re-layouts: 10.1 us -> none  [the longest x1 9.32 us: on_device(): jnp.stack((gate_sum, up_sum, down_sum), axis=2)]
    slice x1 -> x0, local copies, waits for them, and re-layouts: 7.87 us -> none  [on_device(): hidden = values[:, :, 0, :]]
  transfers between devices with their start and end apart: 5 -> 0, of which waited for: 5 -> 0; matrix products, arithmetic and copies ran while one was open for 4% -> 0% of each run, Pallas kernels for 0% -> 0%
where the time goes in v1:
time: 131 us; the launch traced here: 130 us
  Pallas kernels  123 us (94%)
  local copies, waits for them, and re-layouts  6.39 us (5%)
    pallas_call x1, Pallas kernels, on_device(): pl.pallas_call(kernel, out_shape=out_shape, in_specs=[vmem] * 5 + [hbm] *...  123 us
    unnamed x20, local copies, waits for them, and re-layouts  6.39 us

profile of v1, /device:TPU:1, one launch (start us, length us, event | category | flops | bytes accessed | tf_op | source)
XLA Modules:
  0.0 130.4 jit_solution(8676456799147726823)
XLA Ops:
  0.6 0.0 copy-start.5
  0.6 0.9 copy.13.quant_ref
  1.6 0.0 copy-done.5
  1.6 0.0 copy-start.4
  1.6 0.1 copy.14.scale_ref
  1.7 0.7 copy-done.4
  2.4 0.1 copy.15.grad_ref
  2.5 0.0 copy-start
  2.5 0.0 copy-start.1
  2.5 0.0 copy-start.2
  2.5 0.0 copy-start.3
  2.6 1.3 copy.12
  3.9 0.0 copy-done
  3.9 0.0 copy-done.1
  3.9 0.0 copy-done.2
  3.9 0.0 copy-done.3
  3.9 123.3 %shard_map.111 = (bf16[128,224]{1,0:T(8,128)(2,1)S(1)}, bf16[224,1024]{1,0:T(8,128)(2,1)S(1)}, bf16[224,1024]{1,0:T(8,128)(2,1)S(1)}, bf16[1024,224]{1,0:T(8,128)(2,1)S(1)}) custom-call(bf16[128,224]{1,0:T(8,128)(2,1)S(1)} %copy.13.quant_ref, f32[128,56]{1,0:T(8,128)S(1)} %copy.14.scale_ref, bf16[128,224]{1,0:T(8,128)(2,1)S(1)} %copy.15.grad_ref, ...), custom_call_target="tpu_custom_call" | custom-call | flops 1409286144 | bytes 2752512 | tf_op jit(solution)/shard_map/pallas_call | solution.py:390
  127.2 0.7 copy.16
  127.9 1.0 copy.17
  128.9 0.8 copy.20
  129.6 0.8 copy.21
Async XLA Ops:
  0.6 0.9 copy-start.5
  1.6 0.8 copy-start.4
  2.5 1.4 %copy-start = (bf16[1,224,1024]{2,1,0:T(8,128)(2,1)S(1)}, bf16[1,224,1024]{2,1,0:T(8,128)(2,1)}, u32[]{:S(2)}) copy-start(bf16[1,224,1024]{2,1,0:T(8,128)(2,1)} %param.13) | copy-start | bytes 1376260
  2.5 1.3 %copy-start.1 = (bf16[1,224,1024]{2,1,0:T(8,128)(2,1)S(1)}, bf16[1,224,1024]{2,1,0:T(8,128)(2,1)}, u32[]{:S(2)}) copy-start(bf16[1,224,1024]{2,1,0:T(8,128)(2,1)} %param.14) | copy-start | bytes 1376260
  2.5 1.3 %copy-start.2 = (s32[4096,1]{0,1:T(1,128)S(1)}, s32[4096,1]{0,1:T(1,128)}, u32[]{:S(2)}) copy-start(s32[4096,1]{0,1:T(1,128)} %param.11) | copy-start | bytes 49156
  2.5 1.3 %copy-start.3 = (f32[4096,1]{0,1:T(1,128)S(1)}, f32[4096,1]{0,1:T(1,128)}, u32[]{:S(2)}) copy-start(f32[4096,1]{0,1:T(1,128)} %param.12) | copy-start | bytes 49156

commit v2 on v1

v2 whole, which is shorter than its diff:
```python
import functools

import jax
import jax.numpy as jnp
from jax import lax
from jax.experimental import pallas as pl
from jax.experimental.pallas import tpu as pltpu
from jax.sharding import PartitionSpec as P

MESH = pl.DeviceIdType.MESH
F32 = jnp.float32
BF16 = jnp.bfloat16

D = 7168
H = 1024
QB = 128
TOK = 128
CAP = 12
Z = 32
SIDE = 4
W = 224
HALF = H // 2
SLOT = 16
WIDE = 384
ROWS = Z * CAP
CHUNKS = 4
GROUP = Z // CHUNKS
CROWS = GROUP * CAP
BLK = CROWS // SIDE
LANES = HALF // SIDE
MINE = CROWS // 2
TN = ((0,), (0,))
VMEM = 63 * 1024 * 1024


def dot(a, b, dims=((1,), (0,))):
    return lax.dot_general(a, b, (dims, ((), ())), preferred_element_type=F32)


def iota(shape, dim):
    return lax.broadcasted_iota(jnp.int32, shape, dim)


def one_hot(cond):
    return jnp.where(cond, 1.0, 0.0).astype(BF16)


def hop(p):
    return 16 + ((p + 1) // 2) * (1 - 2 * (p % 2))


def to_column(row):
    diag = iota((TOK, TOK), 0) == iota((TOK, TOK), 1)
    spread = jnp.broadcast_to(row, (TOK, TOK))
    return jnp.sum(jnp.where(diag, spread, jnp.zeros_like(spread)), axis=1, keepdims=True)


def sixths(i):
    return i - 6 * ((i * 43) >> 8)


def kernel(
    quant_ref, scale_ref, grad_ref, ids_ref, wts_ref, wg_hbm, wu_hbm, wd_hbm,
    gin_ref, gg_hbm, gu_hbm, gd_hbm,
    gg, gu, gd, send, recv, recvp, wg, wu, wd, wgp, wup, wdp, mg, mu, xo, xp, go, gp,
    part, rx1, sum1, rx2, vals, val, slotp, rslot, rsend, rb,
    zs, zr, fs, fr, ws, wr, wl, cs, cr, ms, mr, ps, pr, bs, br, hs, hr, os,
):
    z = lax.axis_index("expert")
    d = lax.axis_index("dp")
    cx, cy, core = d // 8, (d // 2) % 4, d % 2
    mate = {"dp": d + 1 - 2 * core}

    def at_x(j):
        return {"dp": (((cx + j) % 4) * 4 + cy) * 2 + core}

    def at_y(j):
        return {"dp": (cx * 4 + (cy + j) % 4) * 2 + core}

    def remote(src, dst, s, r, device):
        return pltpu.make_async_remote_copy(
            src_ref=src, dst_ref=dst, send_sem=s, recv_sem=r, device_id=device, device_id_type=MESH
        )

    barrier = pltpu.get_barrier_semaphore()

    def greet(k, carry):
        pl.semaphore_signal(
            barrier, inc=1, device_id={"expert": (z + k) % Z}, device_id_type=MESH
        )
        return carry

    lax.fori_loop(1, Z, greet, 0)
    for device in [mate] + [at_x(j) for j in (1, 2, 3)] + [at_y(j) for j in (1, 2, 3)]:
        pl.semaphore_signal(barrier, inc=1, device_id=device, device_id_type=MESH)

    local = [
        pltpu.make_async_copy(wg_hbm, wg, wl.at[0]),
        pltpu.make_async_copy(wu_hbm, wu, wl.at[1]),
        pltpu.make_async_copy(wd_hbm, wd, wl.at[2]),
    ]
    for c in local:
        c.start()

    ids = ids_ref[pl.ds(z, 1), :]
    member = one_hot(iota((Z, TOK), 0) == jnp.broadcast_to(ids, (Z, TOK)))
    before = one_hot(iota((TOK, TOK), 0) < iota((TOK, TOK), 1))
    earlier = dot(member, before)
    slot = jnp.sum(member.astype(F32) * earlier, axis=0, keepdims=True).astype(jnp.int32)
    k = (ids - z) & (Z - 1)
    p = jnp.where(k < 16, 31 - 2 * k, 2 * k - 32)
    late = jnp.where(slot >= 6, 1, 0)
    sixth = slot - 6 * late
    rows = iota((Z * SLOT, TOK), 0)

    def pickers(base):
        return (
            one_hot(rows == jnp.broadcast_to(base + slot, (Z * SLOT, TOK))),
            one_hot(rows == jnp.broadcast_to(base + CAP + late, (Z * SLOT, TOK))),
        )

    pick_main, pick_tail = pickers(SLOT * p)
    weight = wts_ref[pl.ds(z, 1), :]

    picker = jnp.where(
        iota((W, D // QB), 1) == ((W * d + iota((W, D // QB), 0)) >> 7), 1.0, 0.0
    ).astype(F32)
    col_scale = jnp.dot(
        picker, scale_ref[...], precision=lax.Precision.HIGHEST, preferred_element_type=F32
    )
    x = (quant_ref[...].astype(F32) * col_scale).astype(BF16)
    g = (grad_ref[...].astype(F32) * weight).astype(BF16)
    r, c = iota((W, WIDE), 0), iota((W, WIDE), 1)
    put_x = one_hot(r == c)
    put_g = one_hot(((c >= 256) & (r == c - 256)) | ((c >= W) & (c < 256) & (r == c - 96)))
    put_t = one_hot(r == 160 + (c & 63))
    wide = (dot(x, put_x, TN) + dot(g, put_g, TN)).astype(BF16)
    tail = dot(g, put_t, TN)
    tail = jnp.where((iota((TOK, WIDE), 1) >> 6) == to_column(sixth), tail, 0.0).astype(BF16)
    for q in range(CHUNKS):
        send[pl.ds(128 * q, 128), :] = (
            dot(pick_main[128 * q : 128 * q + 128], wide)
            + dot(pick_tail[128 * q : 128 * q + 128], tail)
        ).astype(BF16)

    pl.semaphore_wait(barrier, Z - 1 + 7)

    def block(q):
        return pl.ds(pl.multiple_of(q * SLOT, SLOT), SLOT)

    def out_copy(q):
        return remote(
            send.at[block(q)], recv.at[block(q)], zs.at[q], zr.at[q],
            {"expert": (z + hop(q)) % Z},
        )

    def start_out(q, carry):
        out_copy(q).start()
        return carry

    lax.fori_loop(0, Z - 1, start_out, 0)
    recv[pl.ds((Z - 1) * SLOT, SLOT), :] = send[pl.ds((Z - 1) * SLOT, SLOT), :]

    other = pl.ds(pl.multiple_of((1 - core) * HALF, HALF), HALF)
    mine = pl.ds(pl.multiple_of(core * HALF, HALF), HALF)
    weights_out = [
        remote(wg.at[:, other], wgp, ws.at[0], wr.at[0], mate),
        remote(wu.at[:, other], wup, ws.at[1], wr.at[1], mate),
        remote(wd.at[:, other], wdp, ws.at[2], wr.at[2], mate),
    ]
    for c in local:
        c.wait()
    for c in weights_out:
        c.start()

    i, j = iota((CROWS, 128), 0), iota((CROWS, 128), 1)
    src, cc = j >> 4, j & 15
    take_main = one_hot((cc < CAP) & (i == CAP * src + cc))
    off = i - CAP * src - 6 * (cc - CAP)
    take_tail = one_hot((cc >= CAP) & (cc < CAP + 2) & (off >= 0) & (off < 6))
    tail_lane = (iota((CROWS, WIDE), 1) >> 6) == sixths(iota((CROWS, WIDE), 0))
    r, c = iota((WIDE, W), 0), iota((WIDE, W), 1)
    get_g = one_hot(((c < 128) & (r == c + 256)) | ((c >= 128) & (c < 160) & (r == c + 96)))
    get_t = one_hot((c >= 160) & (c - 160 == (r & 63)))

    i, j = iota((4 * SLOT, MINE), 0), iota((4 * SLOT, MINE), 1)
    src, cc = i >> 4, i & 15
    lay_main = one_hot((cc < CAP) & (j == CAP * src + cc))
    off = j - CAP * src - 6 * (cc - CAP)
    lay_tail = one_hot((cc >= CAP) & (cc < CAP + 2) & (off >= 0) & (off < 6))
    lay_lane = (iota((MINE, WIDE), 1) >> 6) == sixths(iota((MINE, WIDE), 0))
    repeat = one_hot(iota((64, WIDE), 0) == (iota((64, WIDE), 1) & 63))

    second_core = core.astype(F32)
    r, c = iota((W, HALF), 0), iota((W, HALF), 1)
    lane0 = jnp.where(r == c, 1.0, 0.0)
    lane1 = jnp.where(
        ((c >= W) & (c < 256) & (r == c - 96))
        | ((c >= 256) & (c < WIDE) & (r == c - 256))
        | ((c >= WIDE) & (c < WIDE + 64) & (r == c - W)),
        1.0,
        0.0,
    )
    lane_own = (lane0 + second_core * (lane1 - lane0)).astype(BF16)
    lane_mate = (lane1 + second_core * (lane0 - lane1)).astype(BF16)
    for c in weights_out:
        c.wait_recv()
    mg[...] = (dot(wg[:, mine], lane_own, TN) + dot(wgp[...], lane_mate, TN)).astype(BF16)
    mu[...] = (dot(wu[:, mine], lane_own, TN) + dot(wup[...], lane_mate, TN)).astype(BF16)

    apart = ((p >> 2) + core) & 1
    back_main, back_tail = pickers(SLOT * (16 * apart + 4 * (p >> 3) + (p & 3)))

    first = (cx, cy, cx, cy)
    second = (cy, cx, cy, cx)
    peer1 = (at_x, at_y, at_x, at_y)
    peer2 = (at_y, at_x, at_y, at_x)
    peers = (1, 2, 3)

    def rows_of(t):
        return pl.ds(CROWS * t, CROWS)

    def lanes_of(a):
        return pl.ds(pl.multiple_of(LANES * a, LANES), LANES)

    def blk_of(b):
        return pl.ds(pl.multiple_of(BLK * b, 8), BLK)

    def forward_copy(t):
        at = pl.ds(128 * t, 128)
        return remote(recv.at[at], recvp.at[at], fs.at[t], fr.at[t], mate)

    def rs1(t, j):
        return remote(
            part.at[:, rows_of(t), lanes_of((first[t] + j) % 4)], rx1.at[t, j - 1],
            cs.at[0, t, j - 1], cr.at[0, t, j - 1], peer1[t](j),
        )

    def rs2(t, j):
        return remote(
            sum1.at[t, :, blk_of((second[t] + j) % 4), :], rx2.at[t, j - 1],
            cs.at[1, t, j - 1], cr.at[1, t, j - 1], peer2[t](j),
        )

    def ag2(t, j, back=0):
        ref = vals.at[t, (second[t] + 4 - back) % 4]
        return remote(ref, ref, cs.at[2, t, j - 1], cr.at[2, t, j - 1], peer2[t](j))

    def ag1(t, j, back=0):
        ref = val.at[core, :, rows_of(t), lanes_of((first[t] + 4 - back) % 4)]
        return remote(ref, ref, cs.at[3, t, j - 1], cr.at[3, t, j - 1], peer1[t](j))

    def half_copy(t):
        at = pl.ds(pl.multiple_of(CROWS * t + MINE * (1 - core), 16), MINE)
        return remote(slotp.at[at, :], rslot.at[t], ms.at[t], mr.at[t], mate)

    def pair(t, half):
        ref = val.at[half, :, rows_of(t), :]
        return remote(ref, ref, ps.at[t], pr.at[t], mate)

    def back_copy(u):
        return remote(
            rsend.at[block(u)], rb.at[block(u)], bs.at[u], br.at[u],
            {"expert": (z + Z - hop(8 * (u // 4) + 4 * core + u % 4)) % Z},
        )

    def home_copy(t):
        return remote(
            rb.at[pl.ds(64 * t, 64)], rb.at[pl.ds(256 + 64 * t, 64)], hs.at[t], hr.at[t], mate
        )

    def each(first_one, last_one, act):
        def step(q, carry):
            act(q)
            return carry

        lax.fori_loop(first_one, last_one, step, 0)

    def unpack(ref, t, x_ref, g_ref):
        raw = ref[pl.ds(128 * t, 128), :]
        main = dot(take_main, raw).astype(BF16)
        ends = jnp.where(tail_lane, dot(take_tail, raw), 0.0).astype(BF16)
        x_ref[rows_of(t), :] = main[:, :W]
        g_ref[rows_of(t), :] = (dot(main, get_g) + dot(ends, get_t)).astype(BF16)

    def arrive(t):
        each(GROUP * t, min(GROUP * t + GROUP, Z - 1), lambda q: out_copy(q).wait_recv())
        forward_copy(t).start()

    def products(t):
        at = rows_of(t)
        unpack(recv, t, xo, go)
        forward_copy(t).wait_recv()
        unpack(recvp, t, xp, gp)
        a, b = xo[at, :], xp[at, :]
        part[0, at, :] = (dot(a, wg[:, mine]) + dot(b, wgp[...])).astype(BF16)
        part[1, at, :] = (dot(a, wu[:, mine]) + dot(b, wup[...])).astype(BF16)
        a, b = go[at, :], gp[at, :]
        part[2, at, :] = (dot(a, wd[:, mine]) + dot(b, wdp[...])).astype(BF16)
        for j in peers:
            rs1(t, j).start()

    def add_first(t):
        for j in peers:
            rs1(t, j).wait_recv()
        total = part[:, rows_of(t), lanes_of(first[t])].astype(F32)
        for j in peers:
            total = total + rx1[t, j - 1].astype(F32)
        sum1[t] = total
        for j in peers:
            rs2(t, j).start()

    def gated(t):
        for j in peers:
            rs2(t, j).wait_recv()
        total = sum1[t, :, blk_of(second[t]), :]
        for j in peers:
            total = total + rx2[t, j - 1]
        gate, up, down = total[0], total[1], total[2]
        sigma = jax.nn.sigmoid(gate)
        vals[t, second[t], 0] = gate * sigma * up
        vals[t, second[t], 1] = down * up * sigma * (1.0 + gate * (1.0 - sigma))
        vals[t, second[t], 2] = down * gate * sigma
        for j in peers:
            ag2(t, j).start()

    def gather(t):
        for j in peers:
            ag2(t, j, j).wait_recv()
        for kind in range(3):
            val[core, kind, rows_of(t), lanes_of(first[t])] = jnp.concatenate(
                [vals[t, b, kind] for b in range(SIDE)], axis=0
            ).astype(BF16)
        for j in peers:
            ag1(t, j).start()

    def slots(t):
        for j in peers:
            ag1(t, j, j).wait_recv()
        at = rows_of(t)
        slotp[at, :] = dot(val[core, 1, at, :], mg[...]) + dot(val[core, 2, at, :], mu[...])
        half_copy(t).start()
        pair(t, core).start()

    def give_back(t):
        half_copy(t).wait_recv()
        at = pl.ds(pl.multiple_of(CROWS * t + MINE * core, 16), MINE)
        total = (slotp[at, :] + rslot[t]).astype(BF16)
        ends = jnp.where(lay_lane, dot(total[:, WIDE : WIDE + 64], repeat), 0.0).astype(BF16)
        rsend[pl.ds(64 * t, 64), :] = (
            dot(lay_main, total[:, :WIDE]) + dot(lay_tail, ends)
        ).astype(BF16)
        last = 4 * t + 4 if t < CHUNKS - 1 else 4 * t + 4 - core
        each(4 * t, last, lambda u: back_copy(u).start())

    def come_home(t):
        last = 4 * t + 4 if t < CHUNKS - 1 else 4 * t + 4 - core
        each(4 * t, last, lambda u: back_copy(u).wait_recv())
        home_copy(t).start()

    plan = (
        (arrive, 0), (products, 0), (add_first, 0), (arrive, 1), (products, 1), (gated, 0),
        (arrive, 2), (gather, 0), (products, 2), (arrive, 3), (add_first, 1), (products, 3),
        (slots, 0), (gated, 1), (give_back, 0), (add_first, 2), (add_first, 3), (gather, 1),
        (gated, 2), (gated, 3), (slots, 1), (gather, 2), (give_back, 1), (gather, 3),
        (slots, 2), (give_back, 2), (slots, 3), (give_back, 3),
    )
    for act, t in plan:
        act(t)

    @pl.when(core == 1)
    def _():
        rb[pl.ds(240, SLOT), :] = rsend[pl.ds(240, SLOT), :]

    for t in range(CHUNKS):
        pair(t, 1 - core).wait_recv()
    outs = []
    for t, (ref, out, rows_in, kind) in enumerate(
        ((gg, gg_hbm, xo, 1), (gu, gu_hbm, xo, 2), (gd, gd_hbm, go, 0))
    ):
        come_home(t)
        for h in (0, 1):
            ref[:, pl.ds(HALF * h, HALF)] = dot(rows_in[...], val[h, kind], TN).astype(BF16)
        outs.append(pltpu.make_async_copy(ref, out, os.at[t]))
        outs[t].start()
    come_home(CHUNKS - 1)

    r, c = iota((W, WIDE), 0), iota((W, WIDE), 1)
    lane0 = jnp.where(r == c, 1.0, 0.0)
    lane1 = jnp.where(
        ((r < 128) & (c == r + 256)) | ((r >= 128) & (r < 160) & (c == r + 96)), 1.0, 0.0
    )
    lane2 = jnp.where((r >= 160) & (r - 160 == (c & 63)), 1.0, 0.0)
    from_main = (lane0 + second_core * (lane1 - lane0)).astype(BF16)
    from_tail = (second_core * lane2).astype(BF16)
    for t in range(CHUNKS):
        home_copy(t).wait_recv()
    landed = rb[...]
    main = dot(landed, back_main, TN).astype(BF16)
    ends = jnp.where(
        (iota((WIDE, TOK), 0) >> 6) == jnp.broadcast_to(sixth, (WIDE, TOK)),
        dot(landed, back_tail, TN),
        0.0,
    ).astype(BF16)
    gin_ref[...] = (dot(from_main, main) + dot(from_tail, ends)).astype(BF16)

    each(0, Z - 1, lambda q: out_copy(q).wait_send())
    each(0, 16 - core, lambda u: back_copy(u).wait_send())
    for c in outs:
        c.wait()
    for c in weights_out:
        c.wait_send()
    for t in range(CHUNKS):
        forward_copy(t).wait_send()
        half_copy(t).wait_send()
        pair(t, core).wait_send()
        home_copy(t).wait_send()
        for j in peers:
            rs1(t, j).wait_send()
            rs2(t, j).wait_send()
            ag2(t, j).wait_send()
            ag1(t, j).wait_send()


def copy_out(a, b, c, d, oa, ob, oc, od, sa, sb, sc, sd, come, go):
    held = (sa, sb, sc, sd)
    ins = [pltpu.make_async_copy(r, v, come.at[n]) for n, (r, v) in enumerate(zip((a, b, c, d), held))]
    outs = [pltpu.make_async_copy(v, r, go.at[n]) for n, (v, r) in enumerate(zip(held, (oa, ob, oc, od)))]
    for one in ins:
        one.start()
    for one, two in zip(ins, outs):
        one.wait()
        two.start()
    for two in outs:
        two.wait()


def on_device(quant_in, quant_scale, grad_out, route_ids, route_weights, w_gate, w_up, w_down):
    vmem = pl.BlockSpec(memory_space=pltpu.VMEM)
    anywhere = pl.BlockSpec(memory_space=pl.ANY)
    dma = pltpu.SemaphoreType.DMA
    half = ((W, HALF), BF16)
    whole = ((W, H), BF16)
    packed = ((Z * SLOT, WIDE), BF16)
    dense = ((ROWS, W), BF16)
    shapes = [
        whole, whole, whole, packed, packed, packed, whole, whole, whole, half, half, half,
        ((HALF, HALF), BF16), ((HALF, HALF), BF16), dense, dense, dense, dense,
        ((3, ROWS, HALF), BF16), ((CHUNKS, 3, 3, CROWS, LANES), BF16),
        ((CHUNKS, 3, CROWS, LANES), F32), ((CHUNKS, 3, 3, BLK, LANES), F32),
        ((CHUNKS, SIDE, 3, BLK, LANES), F32), ((2, 3, ROWS, HALF), BF16),
        ((ROWS, HALF), F32), ((CHUNKS, MINE, HALF), F32),
        ((Z * SLOT // 2, WIDE), BF16), packed,
    ]
    four = (CHUNKS,)
    sems = [
        (Z - 1,), (Z - 1,), four, four, (3,), (3,), (3,), (4, CHUNKS, 3), (4, CHUNKS, 3),
        four, four, four, four, (16,), (16,), four, four, (3,),
    ]
    out_shape = [
        jax.ShapeDtypeStruct((W, TOK), BF16),
        jax.ShapeDtypeStruct((W, H), BF16),
        jax.ShapeDtypeStruct((W, H), BF16),
        jax.ShapeDtypeStruct((W, H), BF16),
    ]
    results = pl.pallas_call(
        kernel,
        out_shape=out_shape,
        in_specs=[vmem] * 5 + [anywhere] * 3,
        out_specs=[vmem] + [anywhere] * 3,
        scratch_shapes=[pltpu.VMEM(s, t) for s, t in shapes] + [dma(s) for s in sems],
        compiler_params=pltpu.CompilerParams(
            collective_id=0, has_side_effects=True, vmem_limit_bytes=VMEM
        ),
        cost_estimate=pl.CostEstimate(
            flops=2 * 8 * ROWS * W * H, bytes_accessed=12 * W * H, transcendentals=ROWS * H // 32
        ),
    )(
        quant_in.T, quant_scale.T, grad_out.T,
        route_ids.reshape(Z, TOK), route_weights.reshape(Z, TOK),
        w_gate[0], w_up[0], w_down[0].T,
    )
    gin, gg, gu, gd = pl.pallas_call(
        copy_out,
        out_shape=out_shape,
        in_specs=[anywhere] * 4,
        out_specs=[anywhere] * 4,
        scratch_shapes=[pltpu.VMEM(o.shape, BF16) for o in out_shape] + [dma((4,)), dma((4,))],
        compiler_params=pltpu.CompilerParams(vmem_limit_bytes=VMEM),
        cost_estimate=pl.CostEstimate(flops=0, bytes_accessed=14 * W * H, transcendentals=0),
    )(*results)
    return gin.T, gg[None], gu[None], gd.T[None]


def solution(mesh):
    placed = (
        P("expert", "dp"),
        P("expert", None),
        P("expert", "dp"),
        P(),
        P(),
        P("expert", "dp", None),
        P("expert", "dp", None),
        P("expert", None, "dp"),
    )
    return jax.shard_map(
        on_device,
        mesh=mesh,
        in_specs=placed,
        out_specs=(
            P("expert", "dp"),
            P("expert", "dp", None),
            P("expert", "dp", None),
            P("expert", None, "dp"),
        ),
        check_vma=False,
    )
```

time: 131 us -> 119 us (0.908)
  local copies, waits for them, and re-layouts: 6.39 us -> 0 us
  Pallas kernels: 123 us -> 118 us
    unnamed x20 -> x0, local copies, waits for them, and re-layouts: 6.39 us -> none
    pallas_call x1 -> x2, Pallas kernels: 123 us -> 118 us  [the longest x1 116 us: on_device(): pl.pallas_call(kernel, out_shape=out_shape, in_specs=[vmem] * 5 + [anywhe...]
where the time goes in v2:
time: 119 us
  Pallas kernels  118 us (99%)
    pallas_call x1, Pallas kernels, on_device(): pl.pallas_call(kernel, out_shape=out_shape, in_specs=[vmem] * 5 + [anywhe...  116 us

profile of v2, /device:TPU:1, one launch (start us, length us, event | category | flops | bytes accessed | tf_op | source)
XLA Modules:
  0.0 118.8 jit_solution(12190498532628518625)
XLA Ops:
  0.6 115.9 %shard_map.111 = (bf16[224,128]{1,0:T(8,128)(2,1)}, bf16[224,1024]{1,0:T(8,128)(2,1)}, bf16[224,1024]{1,0:T(8,128)(2,1)}, bf16[224,1024]{1,0:T(8,128)(2,1)}) custom-call(bf16[224,128]{1,0:T(8,128)(2,1)} %bitcast.22, f32[56,128]{1,0:T(8,128)} %bitcast.25, bf16[224,128]{1,0:T(8,128)(2,1)} %bitcast.23, s32[32,128]{1,0:T(8,128)} %bitcast.26, ...), custom_call_target="tpu_custom_call" | custom-call | flops 1409286144 | bytes 2752512 | tf_op jit(solution)/shard_map/pallas_call | solution.py:466
  116.6 2.2 %shard_map.112 = (bf16[224,128]{1,0:T(8,128)(2,1)}, bf16[224,1024]{1,0:T(8,128)(2,1)}, bf16[224,1024]{1,0:T(8,128)(2,1)}, bf16[224,1024]{1,0:T(8,128)(2,1)}) custom-call(bf16[224,128]{1,0:T(8,128)(2,1)} %get-tuple-element.12.a, bf16[224,1024]{1,0:T(8,128)(2,1)} %get-tuple-element.13.b, bf16[224,1024]{1,0:T(8,128)(2,1)} %get-tuple-element.14.c, ...), custom_call_target="tpu_custom_call" | custom-call | bytes 3211264 | tf_op jit(solution)/shard_map/pallas_call | solution.py:483

commit v3 on v2

--- a/solution.py
+++ b/solution.py
@@ -60,11 +60,11 @@
 
 
 def kernel(
-    quant_ref, scale_ref, grad_ref, ids_ref, wts_ref, wg_hbm, wu_hbm, wd_hbm,
+    quant_hbm, scale_hbm, grad_hbm, ids_hbm, wts_hbm, wg_hbm, wu_hbm, wd_hbm,
     gin_ref, gg_hbm, gu_hbm, gd_hbm,
-    gg, gu, gd, send, recv, recvp, wg, wu, wd, wgp, wup, wdp, mg, mu, xo, xp, go, gp,
+    quant_ref, scale_ref, grad_ref, ids_ref, wts_ref, gg, gu, gd, send, recv, recvp, wg, wu, wd, wgp, wup, wdp, mg, mu, xo, xp, go, gp,
     part, rx1, sum1, rx2, vals, val, slotp, rslot, rsend, rb,
-    zs, zr, fs, fr, ws, wr, wl, cs, cr, ms, mr, ps, pr, bs, br, hs, hr, os,
+    zs, zr, fs, fr, ws, wr, wl, cs, cr, ms, mr, ps, pr, bs, br, hs, hr, os, es,
 ):
     z = lax.axis_index("expert")
     d = lax.axis_index("dp")
@@ -94,6 +94,17 @@
     for device in [mate] + [at_x(j) for j in (1, 2, 3)] + [at_y(j) for j in (1, 2, 3)]:
         pl.semaphore_signal(barrier, inc=1, device_id=device, device_id_type=MESH)
 
+    early = [
+        pltpu.make_async_copy(a, b, es.at[n])
+        for n, (a, b) in enumerate(
+            (
+                (ids_hbm, ids_ref), (wts_hbm, wts_ref), (scale_hbm, scale_ref),
+                (quant_hbm, quant_ref), (grad_hbm, grad_ref),
+            )
+        )
+    ]
+    for c in early:
+        c.start()
     local = [
         pltpu.make_async_copy(wg_hbm, wg, wl.at[0]),
         pltpu.make_async_copy(wu_hbm, wu, wl.at[1]),
@@ -102,6 +113,8 @@
     for c in local:
         c.start()
 
+    for c in early:
+        c.wait()
     ids = ids_ref[pl.ds(z, 1), :]
     member = one_hot(iota((Z, TOK), 0) == jnp.broadcast_to(ids, (Z, TOK)))
     before = one_hot(iota((TOK, TOK), 0) < iota((TOK, TOK), 1))
@@ -443,7 +456,9 @@
     whole = ((W, H), BF16)
     packed = ((Z * SLOT, WIDE), BF16)
     dense = ((ROWS, W), BF16)
+    wide_first = ((W, TOK), BF16)
     shapes = [
+        wide_first, ((D // QB, TOK), F32), wide_first, ((Z, TOK), jnp.int32), ((Z, TOK), F32),
         whole, whole, whole, packed, packed, packed, whole, whole, whole, half, half, half,
         ((HALF, HALF), BF16), ((HALF, HALF), BF16), dense, dense, dense, dense,
         ((3, ROWS, HALF), BF16), ((CHUNKS, 3, 3, CROWS, LANES), BF16),
@@ -455,7 +470,7 @@
     four = (CHUNKS,)
     sems = [
         (Z - 1,), (Z - 1,), four, four, (3,), (3,), (3,), (4, CHUNKS, 3), (4, CHUNKS, 3),
-        four, four, four, four, (16,), (16,), four, four, (3,),
+        four, four, four, four, (16,), (16,), four, four, (3,), (5,),
     ]
     out_shape = [
         jax.ShapeDtypeStruct((W, TOK), BF16),
@@ -466,7 +481,7 @@
     results = pl.pallas_call(
         kernel,
         out_shape=out_shape,
-        in_specs=[vmem] * 5 + [anywhere] * 3,
+        in_specs=[anywhere] * 8,
         out_specs=[vmem] + [anywhere] * 3,
         scratch_shapes=[pltpu.VMEM(s, t) for s, t in shapes] + [dma(s) for s in sems],
         compiler_params=pltpu.CompilerParams(

time: 119 us -> 118 us (level)
    pallas_call x1, Pallas kernels: 116 us -> 115 us  [on_device(): pl.pallas_call(kernel, out_shape=out_shape, in_specs=[anywhere] * 8, out_...]
where the time goes in v3:
time: 118 us
  Pallas kernels  117 us (99%)
    pallas_call x1, Pallas kernels, on_device(): pl.pallas_call(kernel, out_shape=out_shape, in_specs=[anywhere] * 8, out_...  115 us

profile of v3, /device:TPU:1, one launch (start us, length us, event | category | flops | bytes accessed | tf_op | source)
XLA Modules:
  0.0 117.6 jit_solution(2602925323129695520)
XLA Ops:
  0.6 114.7 %shard_map.111 = (bf16[224,128]{1,0:T(8,128)(2,1)}, bf16[224,1024]{1,0:T(8,128)(2,1)}, bf16[224,1024]{1,0:T(8,128)(2,1)}, bf16[224,1024]{1,0:T(8,128)(2,1)}) custom-call(bf16[224,128]{1,0:T(8,128)(2,1)} %bitcast.22, f32[56,128]{1,0:T(8,128)} %bitcast.25, bf16[224,128]{1,0:T(8,128)(2,1)} %bitcast.23, s32[32,128]{1,0:T(8,128)} %bitcast.26, ...), custom_call_target="tpu_custom_call" | custom-call | flops 1409286144 | bytes 2752512 | tf_op jit(solution)/shard_map/pallas_call | solution.py:481
  115.4 2.2 %shard_map.112 = (bf16[224,128]{1,0:T(8,128)(2,1)}, bf16[224,1024]{1,0:T(8,128)(2,1)}, bf16[224,1024]{1,0:T(8,128)(2,1)}, bf16[224,1024]{1,0:T(8,128)(2,1)}) custom-call(bf16[224,128]{1,0:T(8,128)(2,1)} %get-tuple-element.12.a, bf16[224,1024]{1,0:T(8,128)(2,1)} %get-tuple-element.13.b, bf16[224,1024]{1,0:T(8,128)(2,1)} %get-tuple-element.14.c, ...), custom_call_target="tpu_custom_call" | custom-call | bytes 3211264 | tf_op jit(solution)/shard_map/pallas_call | solution.py:498
